TPU v7x, 32 devices: a whole 2x2x4 slice. The times are simulated.
32 devices in a mesh: cell: 4 (over y, x), gene: 8 (over z, core).
Axes of the slice: x: 2, y: 2, z: 4, core: 2. Of those that a mesh axis runs over, the one named last changes fastest.
Arguments:
- counts: float32 [1024, 16384], P('cell', 'gene'), as said below
- gene_mean: float32 [16384], P('gene'), may hold values from -5 to 10
- gene_std: float32 [16384], P('gene'), may hold values from 0 to 10
Outputs:
- gram: float32 [16384, 16384], P('gene', 'cell')
Inputs may be any that keep to these rules, and one draw needn't show every extreme that they name: `counts`: whole numbers; every cell has at least one count.
All inputs are finite; a program needn't handle non-finite values.
Results may differ from a plain program's by a relative error of at most 0.013.
Values may be sent and summed in bfloat16 or wider, within the bound.
No kernel may reach another device: no remote copies, remote signals or barrier semaphores. Data moves between devices by JAX's collectives and lax.ppermute only.
A program may use at most 192 MiB of HBM per device.

v0:
```python
import jax
import jax.numpy as jnp
from jax import lax
from jax.sharding import PartitionSpec as P


def standardize(counts, library, gene_mean, gene_std):
    normal = jnp.log1p(counts / library[:, None] * 10000.0)
    spread = jnp.maximum(gene_std, 0.1)
    scaled = jnp.minimum((normal - gene_mean[None, :]) / spread[None, :], 10.0)
    return scaled.astype(jnp.bfloat16)


def shards(counts, gene_mean, gene_std):
    cell_rows = counts.shape[0]
    library = lax.psum(jnp.sum(counts, axis=1), "gene")
    mine = standardize(counts, library, gene_mean, gene_std)
    whole = lax.all_gather(mine, "gene", axis=1, tiled=True)
    groups = lax.axis_size("cell")
    total_cells = cell_rows * groups
    summed = lax.psum_scatter(
        lax.dot_general(
            whole, mine, (((0,), (0,)), ((), ())), preferred_element_type=jnp.float32
        ).astype(jnp.bfloat16),
        "cell",
        scatter_dimension=0,
        tiled=True,
    ).astype(jnp.float32)
    return summed.T / total_cells


def solution(mesh):
    placed = (P("cell", "gene"), P("gene"), P("gene"))
    return jax.shard_map(
        shards, mesh=mesh, in_specs=placed, out_specs=P("gene", "cell"), check_vma=False
    )
```

profile of v0, /device:TPU:0, one launch (start us, length us, event | category | flops | bytes accessed | tf_op | source)
XLA Modules:
  0.0 753.1 jit_solution(6976910526361717398)
XLA Ops:
  6.5 0.0 all-gather.2.cloned.1.call-start
  6.5 1.8 reduce_sum.9
  8.3 18.1 %psum.7 = f32[256]{0:T(256)S(1)} all-reduce(f32[256]{0:T(256)S(1)} %reduce_sum.9), channel_id=1, replica_groups=mesh['cell'=4,'gene'=8] {'gene'}, use_global_device_ids=true, to_apply=%region_1.0 | all-reduce | flops 256 | bytes 2048 | tf_op jit(solution)/shard_map/psum | solution.py:16
  26.4 0.7 broadcast_maximum_fusion
  27.1 3.7 minimum_convert_fusion
  30.7 0.0 all-gather.2.cloned.1.call-update
  30.8 0.0 reduce-scatter.4.cloned.1.call-start
  30.8 80.4 %all-gather.2.cloned.1.call-done = bf16[256,16384]{1,0:T(8,128)(2,1)} async-done(((bf16[256,2048]{1,0:T(8,128)(2,1)}), bf16[256,16384]{1,0:T(8,128)(2,1)}) %all-gather.2.cloned.1.call-update) | async-done | bytes 8388624 | tf_op jit(solution)/shard_map/all_gather | solution.py:18
  111.2 28.2 %convolution_convert_fusion = bf16[16384,2048]{1,0:T(8,128)(2,1)} fusion(bf16[256,16384]{1,0:T(8,128)(2,1)} %all-gather.2.cloned.1.call-done, bf16[256,2048]{1,0:T(8,128)(2,1)} %minimum_convert_fusion), kind=kOutput, calls=%fused_computation | convolution fusion | flops 17213423616 | bytes 76546048 | tf_op jit(solution)/shard_map/dot_general | solution.py:22
  139.4 0.0 reduce-scatter.4.cloned.1.call-update
  139.4 557.0 %reduce-scatter.4.cloned.1.call-done = bf16[4096,2048]{1,0:T(8,128)(2,1)} async-done(((bf16[16384,2048]{1,0:T(8,128)(2,1)}), bf16[4096,2048]{1,0:T(8,128)(2,1)}) %reduce-scatter.4.cloned.1.call-update) | async-done | bytes 16777232
  696.4 18.8 %multiply_bitcast_fusion = f32[2048,4096]{0,1:T(8,128)} fusion(bf16[4096,2048]{1,0:T(8,128)(2,1)} %reduce-scatter.4.cloned.1.call-done), kind=kLoop, calls=%fused_computation.1 | loop fusion | flops 16777216 | bytes 50331648 | tf_op jit(solution)/shard_map/div | solution.py:29
  715.1 31.1 %copy.5 = f32[2048,4096]{1,0:T(8,128)} copy(f32[2048,4096]{0,1:T(8,128)} %multiply_bitcast_fusion) | data formatting | bytes 67108864 | tf_op jit(solution)/shard_map/div | solution.py:29
Async XLA Ops:
  6.5 104.7 %all-gather.2.cloned.1.call-start = ((), (), s32[]{:S(2)}) async-start(), calls=%async_computation.1 | async-start | bytes 9437184 | tf_op jit(solution)/shard_map/all_gather | solution.py:18
  30.8 665.6 %reduce-scatter.4.cloned.1.call-start = ((), (), s32[]{:S(2)}) async-start(), calls=%async_computation.2 | async-start | bytes 83886080
Sparse Core Ops, SparseCore 0:
  30.9 80.2 all-gather.1
  139.5 556.8 reduce-scatter.3
where the time goes:
time: 754 us; the launch traced here: 753 us
  waiting for transfers between devices  637 us (84%)
  local copies, waits for them, and re-layouts  31.1 us (4%)
  matrix products  28.2 us (4%)
  other arithmetic  24.9 us (3%)
  blocking collectives  18.1 us (2%)
  between operations  13.4 us (2%)
    unnamed x3, waiting for transfers between devices  557 us
    all_gather x1, waiting for transfers between devices, shards(): whole = lax.all_gather(mine, 'gene', axis=1, tiled=True)  80.4 us
    div x1, local copies, waits for them, and re-layouts, shards(): return summed.T / total_cells  31.1 us
    dot_general x1, matrix products, shards(): lax.dot_general(whole, mine, (((0,), (0,)), ((), ())), preferred_element_...  28.2 us
    div x1, other arithmetic, shards(): return summed.T / total_cells  18.8 us
    psum x1, blocking collectives, shards(): library = lax.psum(jnp.sum(counts, axis=1), 'gene')  18.1 us
  transfers between devices with their start and end apart: 2, of which 2 were waited for; matrix products, arithmetic and copies ran while one was open for 0% of the time, Pallas kernels for 0%

commit v1 on v0

v1 whole, which is shorter than its diff:
```python
import functools

import jax
import jax.numpy as jnp
import numpy as np
from jax import lax
from jax.experimental import pallas as pl
from jax.experimental.pallas import tpu as pltpu
from jax.sharding import PartitionSpec as P

CHUNKS = 4
HALVES = 2
STRIP = 128
VMEM = pl.BlockSpec(memory_space=pltpu.VMEM)


def send(x, axis, pairs):
    return lax.ppermute(x, axis, pairs)


def count_kernel(counts_ref, out_ref):
    cells, genes = counts_ref.shape
    total = counts_ref[:, :STRIP]
    for at in range(STRIP, genes, STRIP):
        total += counts_ref[:, at : at + STRIP]
    summed = jnp.sum(total, axis=1, keepdims=True)
    flat = jnp.broadcast_to(summed, (cells, STRIP)).T
    out_ref[...] = flat[:8, :]


def count_part(counts):
    cells, genes = counts.shape
    return pl.pallas_call(
        count_kernel,
        in_specs=[VMEM],
        out_specs=VMEM,
        out_shape=jax.ShapeDtypeStruct((8, cells), jnp.float32),
        cost_estimate=pl.CostEstimate(
            flops=cells * genes, bytes_accessed=4 * cells * genes, transcendentals=0
        ),
        name="count_part",
    )(counts)


def library_terms(part, outer, inner):
    total = part
    for s in range(1, inner):
        total = total + send(
            part,
            "gene",
            [
                (o * inner + i, o * inner + (i + s) % inner)
                for o in range(outer)
                for i in range(inner)
            ],
        )
    terms = [total]
    for s in range(1, outer):
        terms.append(
            send(
                total,
                "gene",
                [
                    (o * inner + i, (o + s) % outer * inner + i)
                    for o in range(outer)
                    for i in range(inner)
                ],
            )
        )
    return terms


def standardize_kernel(terms, counts_ref, mean_ref, std_ref, *refs):
    cells, genes = counts_ref.shape
    sums, blocks, rows = (
        refs[:terms],
        refs[terms : terms + CHUNKS],
        refs[terms + CHUNKS :],
    )
    library = sums[0][:1, :]
    for ref in sums[1:]:
        library = library + ref[:1, :]
    factor = jnp.broadcast_to(10000.0 / library, (STRIP, cells)).T
    width, height = genes // CHUNKS, genes // HALVES
    for q in range(CHUNKS):
        half = q * width // height
        start = q * width - half * height

        @pl.loop(0, width // STRIP)
        def _(k):
            there = pl.multiple_of(k * STRIP, STRIP)
            at = pl.ds(q * width + there, STRIP)
            normal = jnp.log1p(counts_ref[:, at] * factor)
            spread = 1.0 / jnp.maximum(std_ref[:, at], 0.1)
            scaled = jnp.minimum((normal - mean_ref[:, at]) * spread, 10.0)
            blocks[q][:, pl.ds(there, STRIP)] = scaled.astype(jnp.bfloat16)
            rows[half][pl.ds(start + there, STRIP), :] = scaled.T.astype(jnp.bfloat16)


def standardize(counts, terms, gene_mean, gene_std):
    cells, genes = counts.shape
    block = jax.ShapeDtypeStruct((cells, genes // CHUNKS), jnp.bfloat16)
    row = jax.ShapeDtypeStruct((genes // HALVES, cells), jnp.bfloat16)
    outs = pl.pallas_call(
        functools.partial(standardize_kernel, len(terms)),
        in_specs=[VMEM] * (3 + len(terms)),
        out_specs=[VMEM] * (CHUNKS + HALVES),
        out_shape=[block] * CHUNKS + [row] * HALVES,
        cost_estimate=pl.CostEstimate(
            flops=20 * cells * genes,
            bytes_accessed=8 * cells * genes,
            transcendentals=cells * genes,
        ),
        name="standardize",
    )(counts, gene_mean[None, :], gene_std[None, :], *terms)
    return outs[:CHUNKS], outs[CHUNKS:]


def line_steps(block, outer, inner):
    ups, downs = [block], [block]
    for h in range(1, outer):
        up = [
            (o * inner + i, (o + 1) * inner + i)
            for o in range(h - 1, outer - 1)
            for i in range(inner)
        ]
        down = [
            (o * inner + i, (o - 1) * inner + i)
            for o in range(1, outer - h + 1)
            for i in range(inner)
        ]
        ups.append(send(ups[-1], "gene", up))
        downs.append(send(downs[-1], "gene", down))
    return ups, downs


def pick_kernel(outer, place_ref, *refs):
    sources = refs[: 2 * outer - 1]
    outs = refs[2 * outer - 1 : 3 * outer - 1]
    sems = refs[3 * outer - 1]
    for j in range(outer):
        for k in range(2 * outer - 1):

            @pl.when(place_ref[j] == k)
            def _():
                pltpu.make_async_copy(sources[k], outs[j], sems.at[j]).start()

    for j in range(outer):
        pltpu.make_async_copy(sources[0], outs[j], sems.at[j]).wait()


def pick(place, ups, downs):
    outer = len(ups)
    sources = list(reversed(downs[1:])) + ups
    shape = jax.ShapeDtypeStruct(ups[0].shape, ups[0].dtype)
    size = ups[0].size * 2
    return pl.pallas_call(
        functools.partial(pick_kernel, outer),
        in_specs=[pl.BlockSpec(memory_space=pltpu.SMEM)]
        + [pl.BlockSpec(memory_space=pl.ANY)] * len(sources),
        out_specs=[pl.BlockSpec(memory_space=pl.ANY)] * outer,
        out_shape=[shape] * outer,
        scratch_shapes=[pltpu.SemaphoreType.DMA((outer,))],
        cost_estimate=pl.CostEstimate(
            flops=0, bytes_accessed=2 * outer * size, transcendentals=0
        ),
        name="pick_blocks",
    )(place, *sources)


def gram_kernel(groups, tiles, scale, place_ref, *refs):
    cols = refs[HALVES * groups : (HALVES + 1) * groups]
    out_ref = refs[-1]
    for half in range(HALVES):
        rows = refs[half * groups : (half + 1) * groups]

        @pl.when(pl.program_id(0) // tiles == half)
        def _():
            total = jnp.dot(
                rows[0][...], cols[0][...], preferred_element_type=jnp.float32
            )
            for j in range(1, groups):
                total += jnp.dot(
                    rows[j][...], cols[j][...], preferred_element_type=jnp.float32
                )
            out_ref[...] = total * scale


def gram_part(gram, column_block, rows, cols, shape, scale):
    groups = len(cols)
    height, depth = rows[0][0].shape
    width = cols[0].shape[1]
    tile = min(512, height)
    tiles = height // tile
    in_specs, operands = [], []
    for half in range(HALVES):
        at = functools.partial(
            lambda half, m, place: (jnp.clip(m - half * tiles, 0, tiles - 1), 0), half
        )
        in_specs += [pl.BlockSpec((tile, depth), at)] * groups
        operands += rows[half]
    in_specs += [pl.BlockSpec((depth, width), lambda m, place: (0, 0))] * groups
    operands += cols
    aliases = {}
    if gram is not None:
        aliases = {1 + len(operands): 0}
        in_specs.append(pl.BlockSpec(memory_space=pl.ANY))
        operands.append(gram)
    return pl.pallas_call(
        functools.partial(gram_kernel, groups, tiles, scale),
        grid_spec=pltpu.PrefetchScalarGridSpec(
            num_scalar_prefetch=1,
            grid=(HALVES * tiles,),
            in_specs=in_specs,
            out_specs=pl.BlockSpec((tile, width), lambda m, place: (m, place[0])),
        ),
        out_shape=jax.ShapeDtypeStruct(shape, jnp.float32),
        input_output_aliases=aliases,
        cost_estimate=pl.CostEstimate(
            flops=2 * groups * shape[0] * depth * width,
            bytes_accessed=4 * shape[0] * width
            + 2 * groups * depth * (shape[0] + width),
            transcendentals=0,
        ),
        name="gram_part",
    )(column_block, *operands)


def row_blocks(mine, groups):
    def cross(x, j):
        return send(x, "cell", [(c, c ^ j) for c in range(groups)])

    if groups != 4:
        return [[x] + [cross(x, j) for j in range(1, groups)] for x in mine]
    a, b = mine
    a1, a2, b1, b2 = cross(a, 1), cross(a, 2), cross(b, 1), cross(b, 2)
    return [[a, a1, a2, cross(a1, 2)], [b, b1, b2, cross(b2, 1)]]


def place_table(groups, outer, inner):
    table = np.zeros((groups, outer * inner, groups + inner), np.int32)
    for c in range(groups):
        for o in range(outer):
            for i in range(inner):
                line = [(c ^ j) for j in range(groups)]
                table[c, o * inner + i] = [outer - 1 + o - to for to in line] + [
                    (i + s) % inner for s in range(inner)
                ]
    return table


def shards(counts, gene_mean, gene_std):
    groups = lax.axis_size("cell")
    outer, inner = groups, lax.axis_size("gene") // groups
    cells, genes = counts.shape
    table = place_table(groups, outer, inner)
    place = jnp.asarray(table)[lax.axis_index("cell"), lax.axis_index("gene")]

    terms = library_terms(count_part(counts), outer, inner)
    blocks, mine = standardize(counts, terms, gene_mean, gene_std)
    rows = row_blocks(mine, groups)

    shape = (genes, genes * inner)
    scale = 1.0 / (cells * groups)
    gram = None
    for q in range(CHUNKS):
        ups, downs = line_steps(blocks[q], outer, inner)
        sends = pick(place[:groups], ups, downs)
        cols = [sends[0]] + [
            send(sends[j], "cell", [(c, c ^ j) for c in range(groups)])
            for j in range(1, groups)
        ]
        for s in range(inner):
            perm = [
                (o * inner + (i + s) % inner, o * inner + i)
                for o in range(outer)
                for i in range(inner)
            ]
            theirs = [send(x, "gene", perm) for x in cols] if s else cols
            column_block = place[groups + s :][:1] * CHUNKS + q
            gram = gram_part(gram, column_block, rows, theirs, shape, scale)
    return gram


def solution(mesh):
    placed = (P("cell", "gene"), P("gene"), P("gene"))
    return jax.shard_map(
        shards, mesh=mesh, in_specs=placed, out_specs=P("gene", "cell"), check_vma=False
    )
```

time: 754 us -> 334 us (0.44)
  waiting for transfers between devices: 637 us -> 52.9 us
  Pallas kernels: 0 us -> 196 us
  starting transfers between devices: 0.04 us -> 75.2 us
  matrix products: 28.2 us -> 0 us
  local copies, waits for them, and re-layouts: 31.1 us -> 5.68 us
  other arithmetic: 24.9 us -> 0.7 us
  blocking collectives: 18.1 us -> 0 us
  between operations: 13.4 us -> 1.88 us
    unnamed x3 -> x0, waiting for transfers between devices: 557 us -> none
    pallas_call x0 -> x14, Pallas kernels: none -> 196 us  [the longest x4 134 us: pick(): pl.pallas_call(functools.partial(pick_kernel, outer), in_specs=[pl.BlockS...]
    all_gather x1 -> x0, waiting for transfers between devices: 80.4 us -> none  [shards(): whole = lax.all_gather(mine, 'gene', axis=1, tiled=True)]
    ppermute x0 -> x62, starting transfers between devices: none -> 75.2 us  [send(): return lax.ppermute(x, axis, pairs)]
    ppermute x0 -> x62, waiting for transfers between devices: none -> 52.9 us  [send(): return lax.ppermute(x, axis, pairs)]
    div x1 -> x0, local copies, waits for them, and re-layouts: 31.1 us -> none  [shards(): return summed.T / total_cells]
    dot_general x1 -> x0, matrix products: 28.2 us -> none  [shards(): lax.dot_general(whole, mine, (((0,), (0,)), ((), ())), preferred_element_...]
    div x1 -> x0, other arithmetic: 18.8 us -> none  [shards(): return summed.T / total_cells]
  transfers between devices with their start and end apart: 2 -> 62, of which waited for: 2 -> 15; matrix products, arithmetic and copies ran while one was open for 0% -> 1% of each run, Pallas kernels for 0% -> 55%
where the time goes in v1:
time: 334 us; the launch traced here: 333 us
  Pallas kernels  196 us (59%)
  starting transfers between devices  75.2 us (23%)
  waiting for transfers between devices  52.9 us (16%)
  local copies, waits for them, and re-layouts  5.68 us (2%)
    pallas_call x4, Pallas kernels, pick(): pl.pallas_call(functools.partial(pick_kernel, outer), in_specs=[pl.BlockS...  134 us
    ppermute x62, starting transfers between devices, send(): return lax.ppermute(x, axis, pairs)  75.2 us
    pallas_call x8, Pallas kernels, gram_part(): pl.pallas_call(functools.partial(gram_kernel, groups, tiles, scale), grid...  54.4 us
    ppermute x62, waiting for transfers between devices, send(): return lax.ppermute(x, axis, pairs)  52.9 us
  transfers between devices with their start and end apart: 62, of which 15 were waited for; matrix products, arithmetic and copies ran while one was open for 1% of the time, Pallas kernels for 55%

profile of v1, /device:TPU:0, one launch (start us, length us, event | category | flops | bytes accessed | tf_op | source)
XLA Modules:
  0.0 332.7 jit_solution(5210676261704469066)
XLA Ops:
  0.0 2.4 count_part.1
  4.6 2.9 collective-permute-start.1
  7.5 2.6 collective-permute-start.2
  12.1 1.6 collective-permute-done.3.refs_3_
  14.3 5.2 %standardize.1 = (bf16[256,512]{1,0:T(8,128)(2,1)}, bf16[256,512]{1,0:T(8,128)(2,1)}, bf16[256,512]{1,0:T(8,128)(2,1)}, bf16[256,512]{1,0:T(8,128)(2,1)}, bf16[1...) custom-call(f32[256,2048]{1,0:T(8,128)} %counts_ref.3, f32[1,2048]{1,0:T(1,128)} %bitcast.6, f32[1,2048]{1,0:T(1,128)} %bitcast.7, ...), custom_call_target="tpu_custom_call" | custom-call | flops 10485760 | bytes 4194304 | tf_op jit(solution)/shard_map/standardize/pallas_call | solution.py:104
  20.8 4.6 %collective-permute-start.52 = (bf16[256,512]{1,0:T(8,128)(2,1)}, bf16[256,512]{1,0:T(8,128)(2,1)S(1)}, u32[]{:S(2)}, u32[]{:S(2)}) collective-permute-start(bf16[256,512]{1,0:T(8,128)(2,1)} %get-tuple-element.44.refs_3_), channel_id=1, source_target_pairs={{0,2},{1,3},{2,4},{3,5},{4,6},{5,7},{8,10},{9,11},{10,12},{11,13},... | collective-permute-start | bytes 786440 | tf_op jit(solution)/shard_map/ppermute | solution.py:18
  26.7 4.6 %collective-permute-start.39 = (bf16[256,512]{1,0:T(8,128)(2,1)}, bf16[256,512]{1,0:T(8,128)(2,1)S(1)}, u32[]{:S(2)}, u32[]{:S(2)}) collective-permute-start(bf16[256,512]{1,0:T(8,128)(2,1)} %get-tuple-element.39.refs_3_), channel_id=1, source_target_pairs={{0,2},{1,3},{2,4},{3,5},{4,6},{5,7},{8,10},{9,11},{10,12},{11,13},... | collective-permute-start | bytes 786440 | tf_op jit(solution)/shard_map/ppermute | solution.py:18
  32.6 4.6 %collective-permute-start.26 = (bf16[256,512]{1,0:T(8,128)(2,1)}, bf16[256,512]{1,0:T(8,128)(2,1)S(1)}, u32[]{:S(2)}, u32[]{:S(2)}) collective-permute-start(bf16[256,512]{1,0:T(8,128)(2,1)} %get-tuple-element.34.refs_3_), channel_id=1, source_target_pairs={{0,2},{1,3},{2,4},{3,5},{4,6},{5,7},{8,10},{9,11},{10,12},{11,13},... | collective-permute-start | bytes 786440 | tf_op jit(solution)/shard_map/ppermute | solution.py:18
  38.5 4.6 %collective-permute-start.13 = (bf16[256,512]{1,0:T(8,128)(2,1)}, bf16[256,512]{1,0:T(8,128)(2,1)S(1)}, u32[]{:S(2)}, u32[]{:S(2)}) collective-permute-start(bf16[256,512]{1,0:T(8,128)(2,1)} %get-tuple-element.29.refs_3_), channel_id=1, source_target_pairs={{0,2},{1,3},{2,4},{3,5},{4,6},{5,7},{8,10},{9,11},{10,12},{11,13},... | collective-permute-start | bytes 786440 | tf_op jit(solution)/shard_map/ppermute | solution.py:18
  54.2 5.4 %collective-permute-done.4.refs_1_ = bf16[1024,256]{1,0:T(8,128)(2,1)S(1)} collective-permute-done((bf16[1024,256]{1,0:T(8,128)(2,1)}, bf16[1024,256]{1,0:T(8,128)(2,1)S(1)}, u32[]{:S(2)}, u32[]{:S(2)}) %collective-permute-start.4) | collective-permute-done | bytes 524320 | tf_op jit(solution)/shard_map/ppermute | solution.py:18
  62.3 4.9 %collective-permute-done.5.refs_2_ = bf16[1024,256]{1,0:T(8,128)(2,1)S(1)} collective-permute-done((bf16[1024,256]{1,0:T(8,128)(2,1)}, bf16[1024,256]{1,0:T(8,128)(2,1)S(1)}, u32[]{:S(2)}, u32[]{:S(2)}) %collective-permute-start.5) | collective-permute-done | bytes 524320 | tf_op jit(solution)/shard_map/ppermute | solution.py:18
  74.9 6.5 %collective-permute-done.11.refs_1_ = bf16[256,512]{1,0:T(8,128)(2,1)S(1)} collective-permute-done((bf16[256,512]{1,0:T(8,128)(2,1)S(1)}, bf16[256,512]{1,0:T(8,128)(2,1)S(1)}, u32[]{:S(2)}, u32[]{:S(2)}) %collective-permute-start.11) | collective-permute-done | bytes 262176 | tf_op jit(solution)/shard_map/ppermute | solution.py:18
  84.1 3.8 %collective-permute-done.51.refs_0_ = bf16[256,512]{1,0:T(8,128)(2,1)} collective-permute-done((bf16[256,512]{1,0:T(8,128)(2,1)}, bf16[256,512]{1,0:T(8,128)(2,1)}, u32[]{:S(2)}, u32[]{:S(2)}) %collective-permute-start.51) | collective-permute-done | bytes 262176 | tf_op jit(solution)/shard_map/ppermute | solution.py:18
  91.2 2.3 collective-permute-done.38.refs_0_
  95.3 33.6 %pick_blocks.7 = (bf16[256,512]{1,0:T(8,128)(2,1)}, bf16[256,512]{1,0:T(8,128)(2,1)}, bf16[256,512]{1,0:T(8,128)(2,1)}, bf16[256,512]{1,0:T(8,128)(2,1)}) custom-call(s32[4]{0:T(128)} %slice_bitcast_fusion.place_ref, bf16[256,512]{1,0:T(8,128)(2,1)} %collective-permute-done.51.refs_0_, bf16[256,512]{1,0:T(8,128)(2,1)} %collective-permute-done.50.refs_1_, ...), custom_call_target="tpu_custom_call" | custom-call | bytes 2097152 | tf_op jit(solution)/shard_map/pick_blocks/pallas_call | solution.py:157
  134.6 10.3 %collective-permute-done.56.refs_9_ = bf16[256,512]{1,0:T(8,128)(2,1)} collective-permute-done((bf16[256,512]{1,0:T(8,128)(2,1)}, bf16[256,512]{1,0:T(8,128)(2,1)}, u32[]{:S(2)}, u32[]{:S(2)}) %collective-permute-start.56) | collective-permute-done | bytes 262176 | tf_op jit(solution)/shard_map/ppermute | solution.py:18
  145.0 33.6 %pick_blocks.6 = (bf16[256,512]{1,0:T(8,128)(2,1)}, bf16[256,512]{1,0:T(8,128)(2,1)}, bf16[256,512]{1,0:T(8,128)(2,1)}, bf16[256,512]{1,0:T(8,128)(2,1)}) custom-call(s32[4]{0:T(128)} %slice_bitcast_fusion.place_ref, bf16[256,512]{1,0:T(8,128)(2,1)} %collective-permute-done.38.refs_0_, bf16[256,512]{1,0:T(8,128)(2,1)} %collective-permute-done.37.refs_1_, ...), custom_call_target="tpu_custom_call" | custom-call | bytes 2097152 | tf_op jit(solution)/shard_map/pick_blocks/pallas_call | solution.py:157
  178.6 33.6 %pick_blocks.5 = (bf16[256,512]{1,0:T(8,128)(2,1)}, bf16[256,512]{1,0:T(8,128)(2,1)}, bf16[256,512]{1,0:T(8,128)(2,1)}, bf16[256,512]{1,0:T(8,128)(2,1)}) custom-call(s32[4]{0:T(128)} %slice_bitcast_fusion.place_ref, bf16[256,512]{1,0:T(8,128)(2,1)} %collective-permute-done.25.refs_0_, bf16[256,512]{1,0:T(8,128)(2,1)} %copy-done.31, ...), custom_call_target="tpu_custom_call" | custom-call | bytes 2097152 | tf_op jit(solution)/shard_map/pick_blocks/pallas_call | solution.py:157
  213.7 2.1 collective-permute-start.47
  216.4 5.3 %collective-permute-done.43.refs_9_ = bf16[256,512]{1,0:T(8,128)(2,1)} collective-permute-done((bf16[256,512]{1,0:T(8,128)(2,1)}, bf16[256,512]{1,0:T(8,128)(2,1)}, u32[]{:S(2)}, u32[]{:S(2)}) %collective-permute-start.43) | collective-permute-done | bytes 262176 | tf_op jit(solution)/shard_map/ppermute | solution.py:18
  222.2 5.1 %collective-permute-done.45.refs_10_ = bf16[256,512]{1,0:T(8,128)(2,1)} collective-permute-done((bf16[256,512]{1,0:T(8,128)(2,1)}, bf16[256,512]{1,0:T(8,128)(2,1)}, u32[]{:S(2)}, u32[]{:S(2)}) %collective-permute-start.45) | collective-permute-done | bytes 262176 | tf_op jit(solution)/shard_map/ppermute | solution.py:18
  229.1 3.8 %collective-permute-done.30.refs_9_ = bf16[256,512]{1,0:T(8,128)(2,1)} collective-permute-done((bf16[256,512]{1,0:T(8,128)(2,1)}, bf16[256,512]{1,0:T(8,128)(2,1)}, u32[]{:S(2)}, u32[]{:S(2)}) %collective-permute-start.30) | collective-permute-done | bytes 262176 | tf_op jit(solution)/shard_map/ppermute | solution.py:18
  234.8 33.6 %pick_blocks.4 = (bf16[256,512]{1,0:T(8,128)(2,1)}, bf16[256,512]{1,0:T(8,128)(2,1)}, bf16[256,512]{1,0:T(8,128)(2,1)}, bf16[256,512]{1,0:T(8,128)(2,1)}) custom-call(s32[4]{0:T(128)} %slice_bitcast_fusion.place_ref, bf16[256,512]{1,0:T(8,128)(2,1)} %collective-permute-done.12.refs_0_, bf16[256,512]{1,0:T(8,128)(2,1)} %copy-done.24, ...), custom_call_target="tpu_custom_call" | custom-call | bytes 2097152 | tf_op jit(solution)/shard_map/pick_blocks/pallas_call | solution.py:157
  268.4 6.8 %gram_part.8.refs_12_ = f32[2048,4096]{1,0:T(8,128)} custom-call(s32[1]{0:T(128)} %bitcast.4.place_ref, bf16[1024,256]{1,0:T(8,128)(2,1)} %get-tuple-element.27.refs_0_, bf16[1024,256]{1,0:T(8,128)(2,1)} %copy-done, bf16[1024,256]{1,0:T(8,128)(2,1)} %copy-done.2, bf16[1024,256]{1,0:T(8,128)(2,1)} %copy-done.4, bf16[1024,256]{1,0:T(8,128)(2,1)} %get-tuple-element.28.refs_4_, ...), custom_call_target="tpu_custom_call" | custom-call | flops 2147483648 | bytes 9437184 | tf_op jit(solution)/shard_map/gram_part/pallas_call | solution.py:209
  276.9 6.8 %gram_part.9.refs_12_ = f32[2048,4096]{1,0:T(8,128)} custom-call(s32[1]{0:T(128)} %bitcast.place_ref, bf16[1024,256]{1,0:T(8,128)(2,1)} %get-tuple-element.27.refs_0_, bf16[1024,256]{1,0:T(8,128)(2,1)} %copy-done, bf16[1024,256]{1,0:T(8,128)(2,1)} %copy-done.2, bf16[1024,256]{1,0:T(8,128)(2,1)} %copy-done.4, ...), custom_call_target="tpu_custom_call", output_to_operand_aliasing={{}: (13, {})} | custom-call | flops 2147483648 | bytes 9437184 | tf_op jit(solution)/shard_map/gram_part/pallas_call | solution.py:209
  283.7 6.8 %gram_part.10.refs_12_ = f32[2048,4096]{1,0:T(8,128)} custom-call(s32[1]{0:T(128)S(6)} %add.35.place_ref, bf16[1024,256]{1,0:T(8,128)(2,1)} %get-tuple-element.27.refs_0_, bf16[1024,256]{1,0:T(8,128)(2,1)} %copy-done, bf16[1024,256]{1,0:T(8,128)(2,1)} %copy-done.2, bf16[1024,256]{1,0:T(8,128)(2,1)} %copy-done.4, ...), custom_call_target="tpu_custom_call", output_to_operand_aliasing={{}: (13, {})} | custom-call | flops 2147483648 | bytes 9437184 | tf_op jit(solution)/shard_map/gram_part/pallas_call | solution.py:209
  291.5 2.1 collective-permute-start.21
  294.9 6.8 %gram_part.11.refs_12_ = f32[2048,4096]{1,0:T(8,128)} custom-call(s32[1]{0:T(128)S(6)} %add.34.place_ref, bf16[1024,256]{1,0:T(8,128)(2,1)} %get-tuple-element.27.refs_0_, bf16[1024,256]{1,0:T(8,128)(2,1)} %copy-done, bf16[1024,256]{1,0:T(8,128)(2,1)} %copy-done.2, bf16[1024,256]{1,0:T(8,128)(2,1)} %copy-done.4, ...), custom_call_target="tpu_custom_call", output_to_operand_aliasing={{}: (13, {})} | custom-call | flops 2147483648 | bytes 9437184 | tf_op jit(solution)/shard_map/gram_part/pallas_call | solution.py:209
  301.7 6.8 %gram_part.12.refs_12_ = f32[2048,4096]{1,0:T(8,128)} custom-call(s32[1]{0:T(128)S(6)} %add.33.place_ref, bf16[1024,256]{1,0:T(8,128)(2,1)} %get-tuple-element.27.refs_0_, bf16[1024,256]{1,0:T(8,128)(2,1)} %copy-done, bf16[1024,256]{1,0:T(8,128)(2,1)} %copy-done.2, bf16[1024,256]{1,0:T(8,128)(2,1)} %copy-done.4, ...), custom_call_target="tpu_custom_call", output_to_operand_aliasing={{}: (13, {})} | custom-call | flops 2147483648 | bytes 9437184 | tf_op jit(solution)/shard_map/gram_part/pallas_call | solution.py:209
  310.7 6.8 %gram_part.13.refs_12_ = f32[2048,4096]{1,0:T(8,128)} custom-call(s32[1]{0:T(128)S(6)} %add.32.place_ref, bf16[1024,256]{1,0:T(8,128)(2,1)} %get-tuple-element.27.refs_0_, bf16[1024,256]{1,0:T(8,128)(2,1)} %copy-done, bf16[1024,256]{1,0:T(8,128)(2,1)} %copy-done.2, bf16[1024,256]{1,0:T(8,128)(2,1)} %copy-done.4, ...), custom_call_target="tpu_custom_call", output_to_operand_aliasing={{}: (13, {})} | custom-call | flops 2147483648 | bytes 9437184 | tf_op jit(solution)/shard_map/gram_part/pallas_call | solution.py:209
  317.5 6.8 %gram_part.14.refs_12_ = f32[2048,4096]{1,0:T(8,128)} custom-call(s32[1]{0:T(128)S(6)} %add.31.place_ref, bf16[1024,256]{1,0:T(8,128)(2,1)} %get-tuple-element.27.refs_0_, bf16[1024,256]{1,0:T(8,128)(2,1)} %copy-done, bf16[1024,256]{1,0:T(8,128)(2,1)} %copy-done.2, bf16[1024,256]{1,0:T(8,128)(2,1)} %copy-done.4, ...), custom_call_target="tpu_custom_call", output_to_operand_aliasing={{}: (13, {})} | custom-call | flops 2147483648 | bytes 9437184 | tf_op jit(solution)/shard_map/gram_part/pallas_call | solution.py:209
  325.9 6.8 %gram_part.15 = f32[2048,4096]{1,0:T(8,128)} custom-call(s32[1]{0:T(128)S(6)} %add.29.place_ref, bf16[1024,256]{1,0:T(8,128)(2,1)} %get-tuple-element.27.refs_0_, bf16[1024,256]{1,0:T(8,128)(2,1)} %copy-done, bf16[1024,256]{1,0:T(8,128)(2,1)} %copy-done.2, bf16[1024,256]{1,0:T(8,128)(2,1)} %copy-done.4, ...), custom_call_target="tpu_custom_call", output_to_operand_aliasing={{}: (13, {})} | custom-call | flops 2147483648 | bytes 9437184 | tf_op jit(solution)/shard_map/gram_part/pallas_call | solution.py:209
  (188 shorter events, 57.5 us)
Async XLA Ops:
  20.8 16.3 %collective-permute-start.52 = (bf16[256,512]{1,0:T(8,128)(2,1)}, bf16[256,512]{1,0:T(8,128)(2,1)S(1)}, u32[]{:S(2)}, u32[]{:S(2)}) collective-permute-start(bf16[256,512]{1,0:T(8,128)(2,1)} %get-tuple-element.44.refs_3_), channel_id=1, source_target_pairs={{0,2},{1,3},{2,4},{3,5},{4,6},{5,7},{8,10},{9,11},{10,12},{11,13},... | collective-permute-start | bytes 786440 | tf_op jit(solution)/shard_map/ppermute | solution.py:18
  26.7 16.4 %collective-permute-start.39 = (bf16[256,512]{1,0:T(8,128)(2,1)}, bf16[256,512]{1,0:T(8,128)(2,1)S(1)}, u32[]{:S(2)}, u32[]{:S(2)}) collective-permute-start(bf16[256,512]{1,0:T(8,128)(2,1)} %get-tuple-element.39.refs_3_), channel_id=1, source_target_pairs={{0,2},{1,3},{2,4},{3,5},{4,6},{5,7},{8,10},{9,11},{10,12},{11,13},... | collective-permute-start | bytes 786440 | tf_op jit(solution)/shard_map/ppermute | solution.py:18
  47.5 19.7 %collective-permute-start.5 = (bf16[1024,256]{1,0:T(8,128)(2,1)}, bf16[1024,256]{1,0:T(8,128)(2,1)S(1)}, u32[]{:S(2)}, u32[]{:S(2)}) collective-permute-start(bf16[1024,256]{1,0:T(8,128)(2,1)} %get-tuple-element.27.refs_0_), channel_id=1, source_target_pairs={{0,16},{8,24},{16,0},{24,8},{1,17},{9,25},{17,1},{25,9},{2,18},{10... | collective-permute-start | bytes 1572872 | tf_op jit(solution)/shard_map/ppermute | solution.py:18
  49.0 18.9 %collective-permute-start.7 = (bf16[1024,256]{1,0:T(8,128)(2,1)}, bf16[1024,256]{1,0:T(8,128)(2,1)S(1)}, u32[]{:S(2)}, u32[]{:S(2)}) collective-permute-start(bf16[1024,256]{1,0:T(8,128)(2,1)} %get-tuple-element.28.refs_4_), channel_id=1, source_target_pairs={{0,8},{8,0},{16,24},{24,16},{1,9},{9,1},{17,25},{25,17},{2,10},{10... | collective-permute-start | bytes 1572872 | tf_op jit(solution)/shard_map/ppermute | solution.py:18
  52.9 16.4 %collective-permute-start.37 = (bf16[256,512]{1,0:T(8,128)(2,1)S(1)}, bf16[256,512]{1,0:T(8,128)(2,1)}, u32[]{:S(2)}, u32[]{:S(2)}) collective-permute-start(bf16[256,512]{1,0:T(8,128)(2,1)S(1)} %collective-permute-done.36.refs_2_), channel_id=1, source_target_pairs={{2,0},{3,1},{4,2},{5,3},{10,8},{11,9},{12,10},{13,11},{18,16},{19,... | collective-permute-start | bytes 786440 | tf_op jit(solution)/shard_map/ppermute | solution.py:18
  70.6 17.2 %collective-permute-start.51 = (bf16[256,512]{1,0:T(8,128)(2,1)}, bf16[256,512]{1,0:T(8,128)(2,1)}, u32[]{:S(2)}, u32[]{:S(2)}) collective-permute-start(bf16[256,512]{1,0:T(8,128)(2,1)} %collective-permute-done.50.refs_1_), channel_id=1, source_target_pairs={{2,0},{3,1},{10,8},{11,9},{18,16},{19,17},{26,24},{27,25}} | collective-permute-start | bytes 786440 | tf_op jit(solution)/shard_map/ppermute | solution.py:18
  72.2 17.7 %collective-permute-start.54 = (bf16[256,512]{1,0:T(8,128)(2,1)}, bf16[256,512]{1,0:T(8,128)(2,1)}, u32[]{:S(2)}, u32[]{:S(2)}) collective-permute-start(bf16[256,512]{1,0:T(8,128)(2,1)} %collective-permute-done.53.refs_5_), channel_id=1, source_target_pairs={{4,6},{5,7},{12,14},{13,15},{20,22},{21,23},{28,30},{29,31}} | collective-permute-start | bytes 786440 | tf_op jit(solution)/shard_map/ppermute | solution.py:18
  73.5 19.9 %collective-permute-start.38 = (bf16[256,512]{1,0:T(8,128)(2,1)}, bf16[256,512]{1,0:T(8,128)(2,1)}, u32[]{:S(2)}, u32[]{:S(2)}) collective-permute-start(bf16[256,512]{1,0:T(8,128)(2,1)} %collective-permute-done.37.refs_1_), channel_id=1, source_target_pairs={{2,0},{3,1},{10,8},{11,9},{18,16},{19,17},{26,24},{27,25}} | collective-permute-start | bytes 786440 | tf_op jit(solution)/shard_map/ppermute | solution.py:18
  81.4 47.5 %collective-permute-start.41 = (bf16[256,512]{1,0:T(8,128)(2,1)}, bf16[256,512]{1,0:T(8,128)(2,1)}, u32[]{:S(2)}, u32[]{:S(2)}) collective-permute-start(bf16[256,512]{1,0:T(8,128)(2,1)} %copy-done.32), channel_id=1, source_target_pairs={{4,6},{5,7},{12,14},{13,15},{20,22},{21,23},{28,30},{29,31}} | collective-permute-start | bytes 786440 | tf_op jit(solution)/shard_map/ppermute | solution.py:18
  82.8 47.8 %collective-permute-start.25 = (bf16[256,512]{1,0:T(8,128)(2,1)}, bf16[256,512]{1,0:T(8,128)(2,1)}, u32[]{:S(2)}, u32[]{:S(2)}) collective-permute-start(bf16[256,512]{1,0:T(8,128)(2,1)} %copy-done.31), channel_id=1, source_target_pairs={{2,0},{3,1},{10,8},{11,9},{18,16},{19,17},{26,24},{27,25}} | collective-permute-start | bytes 786440 | tf_op jit(solution)/shard_map/ppermute | solution.py:18
  87.8 43.3 %collective-permute-start.28 = (bf16[256,512]{1,0:T(8,128)(2,1)}, bf16[256,512]{1,0:T(8,128)(2,1)}, u32[]{:S(2)}, u32[]{:S(2)}) collective-permute-start(bf16[256,512]{1,0:T(8,128)(2,1)} %copy-done.33), channel_id=1, source_target_pairs={{4,6},{5,7},{12,14},{13,15},{20,22},{21,23},{28,30},{29,31}} | collective-permute-start | bytes 786440 | tf_op jit(solution)/shard_map/ppermute | solution.py:18
  89.9 42.8 %collective-permute-start.12 = (bf16[256,512]{1,0:T(8,128)(2,1)S(1)}, bf16[256,512]{1,0:T(8,128)(2,1)}, u32[]{:S(2)}, u32[]{:S(2)}) collective-permute-start(bf16[256,512]{1,0:T(8,128)(2,1)S(1)} %collective-permute-done.11.refs_1_), channel_id=1, source_target_pairs={{2,0},{3,1},{10,8},{11,9},{18,16},{19,17},{26,24},{27,25}} | collective-permute-start | bytes 786440 | tf_op jit(solution)/shard_map/ppermute | solution.py:18
  93.4 39.7 %collective-permute-start.15 = (bf16[256,512]{1,0:T(8,128)(2,1)}, bf16[256,512]{1,0:T(8,128)(2,1)}, u32[]{:S(2)}, u32[]{:S(2)}) collective-permute-start(bf16[256,512]{1,0:T(8,128)(2,1)} %collective-permute-done.14.refs_5_), channel_id=1, source_target_pairs={{4,6},{5,7},{12,14},{13,15},{20,22},{21,23},{28,30},{29,31}} | collective-permute-start | bytes 786440 | tf_op jit(solution)/shard_map/ppermute | solution.py:18
  128.9 84.7 %collective-permute-start.6 = (bf16[1024,256]{1,0:T(8,128)(2,1)S(1)}, bf16[1024,256]{1,0:T(8,128)(2,1)S(1)}, u32[]{:S(2)}, u32[]{:S(2)}) collective-permute-start(bf16[1024,256]{1,0:T(8,128)(2,1)S(1)} %collective-permute-done.4.refs_1_), channel_id=1, source_target_pairs={{0,16},{8,24},{16,0},{24,8},{1,17},{9,25},{17,1},{25,9},{2,18},{10... | collective-permute-start | bytes 1572872 | tf_op jit(solution)/shard_map/ppermute | solution.py:18
  130.5 85.2 %collective-permute-start.9 = (bf16[1024,256]{1,0:T(8,128)(2,1)S(1)}, bf16[1024,256]{1,0:T(8,128)(2,1)S(1)}, u32[]{:S(2)}, u32[]{:S(2)}) collective-permute-start(bf16[1024,256]{1,0:T(8,128)(2,1)S(1)} %collective-permute-done.8.refs_6_), channel_id=1, source_target_pairs={{0,8},{8,0},{16,24},{24,16},{1,9},{9,1},{17,25},{25,17},{2,10},{10... | collective-permute-start | bytes 1572872 | tf_op jit(solution)/shard_map/ppermute | solution.py:18
  132.6 79.5 %collective-permute-start.58 = (bf16[256,512]{1,0:T(8,128)(2,1)}, bf16[256,512]{1,0:T(8,128)(2,1)}, u32[]{:S(2)}, u32[]{:S(2)}) collective-permute-start(bf16[256,512]{1,0:T(8,128)(2,1)} %get-tuple-element.47), channel_id=1, source_target_pairs={{0,16},{8,24},{16,0},{24,8},{1,17},{9,25},{17,1},{25,9},{2,18},{10... | collective-permute-start | bytes 786440 | tf_op jit(solution)/shard_map/ppermute | solution.py:18
  133.1 79.6 %collective-permute-start.60 = (bf16[256,512]{1,0:T(8,128)(2,1)}, bf16[256,512]{1,0:T(8,128)(2,1)}, u32[]{:S(2)}, u32[]{:S(2)}) collective-permute-start(bf16[256,512]{1,0:T(8,128)(2,1)} %get-tuple-element.48), channel_id=1, source_target_pairs={{0,24},{8,16},{16,8},{24,0},{1,25},{9,17},{17,9},{25,1},{2,26},{10... | collective-permute-start | bytes 786440 | tf_op jit(solution)/shard_map/ppermute | solution.py:18
  145.0 70.8 %collective-permute-start.55 = (bf16[256,512]{1,0:T(8,128)(2,1)}, bf16[256,512]{1,0:T(8,128)(2,1)}, u32[]{:S(2)}, u32[]{:S(2)}) collective-permute-start(bf16[256,512]{1,0:T(8,128)(2,1)} %get-tuple-element.45.refs_8_), channel_id=1, source_target_pairs={{1,0},{0,1},{3,2},{2,3},{5,4},{4,5},{7,6},{6,7},{9,8},{8,9},{11,10... | collective-permute-start | bytes 786440 | tf_op jit(solution)/shard_map/ppermute | solution.py:18
  215.8 17.2 %collective-permute-start.30 = (bf16[256,512]{1,0:T(8,128)(2,1)}, bf16[256,512]{1,0:T(8,128)(2,1)}, u32[]{:S(2)}, u32[]{:S(2)}) collective-permute-start(bf16[256,512]{1,0:T(8,128)(2,1)} %get-tuple-element.36), channel_id=1, source_target_pairs={{0,8},{8,0},{16,24},{24,16},{1,9},{9,1},{17,25},{25,17},{2,10},{10... | collective-permute-start | bytes 786440 | tf_op jit(solution)/shard_map/ppermute | solution.py:18
  221.7 53.5 %collective-permute-start.32 = (bf16[256,512]{1,0:T(8,128)(2,1)}, bf16[256,512]{1,0:T(8,128)(2,1)}, u32[]{:S(2)}, u32[]{:S(2)}) collective-permute-start(bf16[256,512]{1,0:T(8,128)(2,1)} %get-tuple-element.37), channel_id=1, source_target_pairs={{0,16},{8,24},{16,0},{24,8},{1,17},{9,25},{17,1},{25,9},{2,18},{10... | collective-permute-start | bytes 786440 | tf_op jit(solution)/shard_map/ppermute | solution.py:18
  227.3 48.5 %collective-permute-start.34 = (bf16[256,512]{1,0:T(8,128)(2,1)}, bf16[256,512]{1,0:T(8,128)(2,1)}, u32[]{:S(2)}, u32[]{:S(2)}) collective-permute-start(bf16[256,512]{1,0:T(8,128)(2,1)} %get-tuple-element.38), channel_id=1, source_target_pairs={{0,24},{8,16},{16,8},{24,0},{1,25},{9,17},{17,9},{25,1},{2,26},{10... | collective-permute-start | bytes 786440 | tf_op jit(solution)/shard_map/ppermute | solution.py:18
  228.6 47.7 %collective-permute-start.57 = (bf16[256,512]{1,0:T(8,128)(2,1)}, bf16[256,512]{1,0:T(8,128)(2,1)}, u32[]{:S(2)}, u32[]{:S(2)}) collective-permute-start(bf16[256,512]{1,0:T(8,128)(2,1)} %collective-permute-done.56.refs_9_), channel_id=1, source_target_pairs={{1,0},{0,1},{3,2},{2,3},{5,4},{4,5},{7,6},{6,7},{9,8},{8,9},{11,10... | collective-permute-start | bytes 786440 | tf_op jit(solution)/shard_map/ppermute | solution.py:18
  228.6 47.7 %collective-permute-start.59 = (bf16[256,512]{1,0:T(8,128)(2,1)}, bf16[256,512]{1,0:T(8,128)(2,1)}, u32[]{:S(2)}, u32[]{:S(2)}) collective-permute-start(bf16[256,512]{1,0:T(8,128)(2,1)} %collective-permute-done.58.refs_10_), channel_id=1, source_target_pairs={{1,0},{0,1},{3,2},{2,3},{5,4},{4,5},{7,6},{6,7},{9,8},{8,9},{11,10... | collective-permute-start | bytes 786440 | tf_op jit(solution)/shard_map/ppermute | solution.py:18
  232.9 43.9 %collective-permute-start.61 = (bf16[256,512]{1,0:T(8,128)(2,1)}, bf16[256,512]{1,0:T(8,128)(2,1)}, u32[]{:S(2)}, u32[]{:S(2)}) collective-permute-start(bf16[256,512]{1,0:T(8,128)(2,1)} %collective-permute-done.60.refs_11_), channel_id=1, source_target_pairs={{1,0},{0,1},{3,2},{2,3},{5,4},{4,5},{7,6},{6,7},{9,8},{8,9},{11,10... | collective-permute-start | bytes 786440 | tf_op jit(solution)/shard_map/ppermute | solution.py:18
  275.8 15.7 %collective-permute-start.17 = (bf16[256,512]{1,0:T(8,128)(2,1)}, bf16[256,512]{1,0:T(8,128)(2,1)S(1)}, u32[]{:S(2)}, u32[]{:S(2)}) collective-permute-start(bf16[256,512]{1,0:T(8,128)(2,1)} %get-tuple-element.31), channel_id=1, source_target_pairs={{0,8},{8,0},{16,24},{24,16},{1,9},{9,1},{17,25},{25,17},{2,10},{10... | collective-permute-start | bytes 786440 | tf_op jit(solution)/shard_map/ppermute | solution.py:18
  276.3 17.3 %collective-permute-start.44 = (bf16[256,512]{1,0:T(8,128)(2,1)}, bf16[256,512]{1,0:T(8,128)(2,1)S(1)}, u32[]{:S(2)}, u32[]{:S(2)}) collective-permute-start(bf16[256,512]{1,0:T(8,128)(2,1)} %collective-permute-done.43.refs_9_), channel_id=1, source_target_pairs={{1,0},{0,1},{3,2},{2,3},{5,4},{4,5},{7,6},{6,7},{9,8},{8,9},{11,10... | collective-permute-start | bytes 786440 | tf_op jit(solution)/shard_map/ppermute | solution.py:18
  276.3 17.3 %collective-permute-start.46 = (bf16[256,512]{1,0:T(8,128)(2,1)}, bf16[256,512]{1,0:T(8,128)(2,1)S(1)}, u32[]{:S(2)}, u32[]{:S(2)}) collective-permute-start(bf16[256,512]{1,0:T(8,128)(2,1)} %collective-permute-done.45.refs_10_), channel_id=1, source_target_pairs={{1,0},{0,1},{3,2},{2,3},{5,4},{4,5},{7,6},{6,7},{9,8},{8,9},{11,10... | collective-permute-start | bytes 786440 | tf_op jit(solution)/shard_map/ppermute | solution.py:18
  276.8 17.3 %collective-permute-start.48 = (bf16[256,512]{1,0:T(8,128)(2,1)}, bf16[256,512]{1,0:T(8,128)(2,1)S(1)}, u32[]{:S(2)}, u32[]{:S(2)}) collective-permute-start(bf16[256,512]{1,0:T(8,128)(2,1)} %collective-permute-done.47.refs_11_), channel_id=1, source_target_pairs={{1,0},{0,1},{3,2},{2,3},{5,4},{4,5},{7,6},{6,7},{9,8},{8,9},{11,10... | collective-permute-start | bytes 786440 | tf_op jit(solution)/shard_map/ppermute | solution.py:18
  290.5 18.0 %collective-permute-start.19 = (bf16[256,512]{1,0:T(8,128)(2,1)}, bf16[256,512]{1,0:T(8,128)(2,1)S(1)}, u32[]{:S(2)}, u32[]{:S(2)}) collective-permute-start(bf16[256,512]{1,0:T(8,128)(2,1)} %get-tuple-element.32), channel_id=1, source_target_pairs={{0,16},{8,24},{16,0},{24,8},{1,17},{9,25},{17,1},{25,9},{2,18},{10... | collective-permute-start | bytes 786440 | tf_op jit(solution)/shard_map/ppermute | solution.py:18
  291.5 17.2 %collective-permute-start.21 = (bf16[256,512]{1,0:T(8,128)(2,1)S(1)}, bf16[256,512]{1,0:T(8,128)(2,1)S(1)}, u32[]{:S(2)}, u32[]{:S(2)}) collective-permute-start(bf16[256,512]{1,0:T(8,128)(2,1)S(1)} %copy-done.38), channel_id=1, source_target_pairs={{0,24},{8,16},{16,8},{24,0},{1,25},{9,17},{17,9},{25,1},{2,26},{10... | collective-permute-start | bytes 786440 | tf_op jit(solution)/shard_map/ppermute | solution.py:18
  308.5 15.8 %collective-permute-start.16 = (bf16[256,512]{1,0:T(8,128)(2,1)S(1)}, bf16[256,512]{1,0:T(8,128)(2,1)S(1)}, u32[]{:S(2)}, u32[]{:S(2)}) collective-permute-start(bf16[256,512]{1,0:T(8,128)(2,1)S(1)} %copy-done.7), channel_id=1, source_target_pairs={{1,0},{0,1},{3,2},{2,3},{5,4},{4,5},{7,6},{6,7},{9,8},{8,9},{11,10... | collective-permute-start | bytes 786440 | tf_op jit(solution)/shard_map/ppermute | solution.py:18
  308.7 15.6 %collective-permute-start.18 = (bf16[256,512]{1,0:T(8,128)(2,1)S(1)}, bf16[256,512]{1,0:T(8,128)(2,1)S(1)}, u32[]{:S(2)}, u32[]{:S(2)}) collective-permute-start(bf16[256,512]{1,0:T(8,128)(2,1)S(1)} %collective-permute-done.17.refs_9_), channel_id=1, source_target_pairs={{1,0},{0,1},{3,2},{2,3},{5,4},{4,5},{7,6},{6,7},{9,8},{8,9},{11,10... | collective-permute-start | bytes 786440 | tf_op jit(solution)/shard_map/ppermute | solution.py:18
  (69 other events, 1994.8 us)
